TPU v7x, 32 devices: a whole 2x2x4 slice. The times are simulated.
32 devices in a mesh: groups: 2 (over x), row: 4 (over y, core), col: 4 (over z).
Axes of the slice: x: 2, y: 2, z: 4, core: 2. Of those that a mesh axis runs over, the one named last changes fastest.
Arguments:
- embedding: bfloat16 [1024, 64, 128], P(('groups', 'row', 'col')), parts along dimension 0, may hold values from -6 to 6
- combined: float32 [1024, 64, 128], P(('groups', 'col', 'row')), parts along dimension 0, may hold values from -6 to 6
- blocks: bfloat16 [32, 256, 128, 128], P(('groups', 'row', 'col')), parts along dimension 0, may hold values from 0 to 1
- block_rows: int32 [32, 256], P(('groups', 'row', 'col')), parts along dimension 0, may hold values from 0 to 127
- block_cols: int32 [32, 256], P(('groups', 'row', 'col')), parts along dimension 0, may hold values from 0 to 127, as said below
- block_counts: int32 [32], P(('groups', 'row', 'col')), parts along dimension 0, may hold values from 64 to 256, as said below
- degrees: int32 [131072], P('groups'), parts along dimension 0, may hold values from 8 to 128
Outputs:
- next_layer: bfloat16 [1024, 64, 128], P(('groups', 'col', 'row')), parts along dimension 0
- combined_out: float32 [1024, 64, 128], P(('groups', 'col', 'row')), parts along dimension 0
There are 2 independent parts, one for each index of `groups`. A program takes and returns all parts, laid end to end along the dimension named above; each array names one. Nothing has to cross between parts.
Inputs may be any that keep to these rules, and one draw needn't show every extreme that they name: `block_counts`: some tile's list holds exactly 256 live blocks. `block_cols`: in each tile's list, at most 64 slots (live or not) name block columns of one share s, the columns s * 32 to (s + 1) * 32 - 1, and in every tile some share is named by exactly 64 slots.
All inputs are finite; a program needn't handle non-finite values.
Results may differ from a plain program's by a relative error of at most 0.0049.
Values may be sent and summed in bfloat16 or wider, within the bound.
A program may use at most 128 MiB of HBM per device.

v0:
```python
import jax
import jax.numpy as jnp
from jax import lax
from jax.sharding import PartitionSpec as P


def slot_terms(sources, own_tiles, src_blocks, alive_mask):
    source_rows = sources.shape[0]
    width = sources.shape[1]
    lane_count = sources.shape[2]
    slot_total = src_blocks.shape[0]
    pick_table = (src_blocks[:, None] == jnp.arange(source_rows, dtype=jnp.int32)[None, :]).astype(
        jnp.bfloat16
    )
    picked = jnp.dot(
        pick_table,
        sources.reshape(source_rows, width * lane_count),
        preferred_element_type=jnp.float32,
    )
    picked = picked.astype(jnp.bfloat16).reshape(slot_total, width, lane_count)
    products = jnp.einsum("kwr,krc->kwc", picked, own_tiles, preferred_element_type=jnp.float32)
    return jnp.where(alive_mask[:, None, None], products, jnp.zeros_like(products))


def shards(embedding, combined, blocks, block_rows, block_cols, block_counts, degrees):
    n_row = lax.axis_size("row")
    n_col = lax.axis_size("col")
    row_index = lax.axis_index("row")
    col_index = lax.axis_index("col")
    own_blocks = embedding.shape[0]
    lane_count = embedding.shape[2]
    width = embedding.shape[1]
    col_blocks = own_blocks * n_row
    inv_root = (1.0 / jnp.sqrt(degrees.astype(jnp.float32))).reshape(-1, 1, lane_count)
    src_scale = lax.dynamic_slice_in_dim(
        inv_root, (row_index * n_col + col_index) * own_blocks, own_blocks, 0
    )
    scaled = (embedding.astype(jnp.float32) * src_scale).astype(jnp.bfloat16)
    gathered = lax.all_gather(scaled, "col", axis=0, tiled=True)
    own_tiles = blocks[0]
    src_blocks = block_rows[0]
    dst_blocks = block_cols[0]
    own_count = block_counts[0]
    slot_total = own_tiles.shape[0]
    slot_ids = jnp.arange(slot_total, dtype=jnp.int32)
    products = slot_terms(gathered, own_tiles, src_blocks, slot_ids < own_count)
    flat_products = products.reshape(slot_total, width * lane_count)
    dst_table = (dst_blocks[None, :] == jnp.arange(col_blocks, dtype=jnp.int32)[:, None]).astype(
        jnp.float32
    )
    partial_value = jnp.dot(
        dst_table,
        flat_products,
        precision=lax.Precision.HIGHEST,
        preferred_element_type=jnp.float32,
    )
    partial_value = partial_value.reshape(col_blocks, width, lane_count)
    summed = lax.psum_scatter(partial_value, "row", scatter_dimension=0, tiled=True)
    dst_scale = lax.dynamic_slice_in_dim(
        inv_root, (col_index * n_row + row_index) * own_blocks, own_blocks, 0
    )
    update = summed * dst_scale
    return (update.astype(jnp.bfloat16), combined + update)


def solution(mesh):
    return jax.shard_map(
        shards,
        mesh=mesh,
        in_specs=(
            P(("groups", "row", "col"), None, None),
            P(("groups", "col", "row"), None, None),
            P(("groups", "row", "col"), None, None, None),
            P(("groups", "row", "col"), None),
            P(("groups", "row", "col"), None),
            P(("groups", "row", "col")),
            P("groups"),
        ),
        out_specs=(
            P(("groups", "col", "row"), None, None),
            P(("groups", "col", "row"), None, None),
        ),
        check_vma=False,
    )
```

profile of v0, /device:TPU:0, one launch (start us, length us, event | category | flops | bytes accessed | tf_op | source)
XLA Modules:
  0.0 153.2 jit_solution(15473321476553325440)
XLA Ops:
  7.2 0.0 all-gather.2.cloned.1.call-start
  7.2 1.0 rsqrt_bitcast_fusion
  8.2 2.0 %multiply_convert_fusion = bf16[32,64,128]{2,1,0:T(8,128)(2,1)} fusion(bf16[32,64,128]{2,1,0:T(8,128)(2,1)} %param.7, f32[32,128]{1,0:T(8,128)S(1)} %get-tuple-element.9), kind=kLoop, calls=%fused_computation.9 | loop fusion | flops 786432 | bytes 1064960 | tf_op jit(solution)/shard_map/convert_element_type | solution.py:38
  10.2 0.0 all-gather.2.cloned.1.call-update
  10.3 0.0 reduce-scatter.2.cloned.1.call-start
  11.0 48.1 %all-gather.2.cloned.1.call-done = bf16[128,64,128]{2,1,0:T(8,128)(2,1)} async-done(((bf16[32,64,128]{2,1,0:T(8,128)(2,1)}), bf16[128,64,128]{2,1,0:T(8,128)(2,1)}) %all-gather.2.cloned.1.call-update) | async-done | bytes 2097168 | tf_op jit(solution)/shard_map/all_gather | solution.py:39
  59.0 3.4 %fusion.4 = bf16[32,8,64,128]{3,1,2,0:T(8,128)(2,1)S(1)} fusion(bf16[16,8,64,128]{3,2,1,0:T(8,128)(2,1)} %bitcast.39, s32[256]{0:T(256)} %bitcast.40), kind=kOutput, calls=%fused_computation.5 | convolution fusion | flops 539000832 | bytes 6292480 | tf_op jit(solution)/shard_map/dot_general | solution.py:15
  62.5 1.2 copy.18
  63.7 4.7 %broadcast_select_fusion = f32[256,64,128]{2,1,0:T(8,128)S(1)} fusion(pred[256]{0:T(512)(128)(4,1)S(1)} %iota_compare_fusion.3, bf16[256,64,128]{2,1,0:T(8,128)(2,1)S(1)} %bitcast.36, bf16[1,256,128,128]{3,2,1,0:T(8,128)(2,1)} %param.9), kind=kOutput, calls=%fused_computation.4 | convolution fusion | flops 538968064 | bytes 20971776 | tf_op jit(solution)/shard_map/kwr,krc->kwc/dot_general | solution.py:21
  68.4 10.9 %copy.26 = f32[32,8,64,128]{3,1,2,0:T(8,128)} copy(f32[32,8,64,128]{3,2,1,0:T(8,128)S(1)} %bitcast.35) | data formatting | bytes 16777216
  79.3 0.0 copy-start.1
  79.3 9.0 %copy.13 = f32[8192,256]{1,0:T(8,128)} copy(f32[8192,256]{0,1:T(8,128)} %bitcast.37) | data formatting | bytes 16777216 | tf_op jit(solution)/shard_map/dot_general | solution.py:51
  88.3 0.0 copy-done.1
  88.3 0.0 copy-start
  88.3 10.2 %fusion.8 = f32[128,64,128]{2,0,1:T(8,128)} fusion(f32[64,128,256]{2,1,0:T(8,128)} %bitcast.38, s32[256]{0:T(256)S(1)} %bitcast.41), kind=kOutput, calls=%fused_computation.15 | convolution fusion | flops 3221258240 | bytes 12583936 | tf_op jit(solution)/shard_map/dot_general | solution.py:51
  98.5 0.0 reduce-scatter.2.cloned.1.call-update
  98.5 43.4 %reduce-scatter.2.cloned.1.call-done = f32[32,64,128]{2,0,1:T(8,128)} async-done(((f32[128,64,128]{2,0,1:T(8,128)}), f32[32,64,128]{2,0,1:T(8,128)}) %reduce-scatter.2.cloned.1.call-update) | async-done | bytes 1048592 | tf_op jit(solution)/shard_map/reduce_scatter | solution.py:58
  141.9 0.0 copy-done
  141.9 1.9 %copy_add_fusion = (f32[32,64,128]{2,0,1:T(8,128)S(1)}, bf16[32,64,128]{2,0,1:T(8,128)(2,1)S(1)}) fusion(f32[32,64,128]{2,1,0:T(8,128)S(1)} %copy-done, f32[32,64,128]{2,0,1:T(8,128)} %reduce-scatter.2.cloned.1.call-done, f32[32,128]{1,0:T(8,128)S(1)} %get-tuple-element.8), kind=kLoop, calls=%fused_computation.8 | loop fusion | flops 786432 | bytes 3686400 | tf_op jit(solution)/shard_map/add | solution.py:63
  143.8 1.6 %copy.16 = f32[32,64,128]{2,1,0:T(8,128)} copy(f32[32,64,128]{2,0,1:T(8,128)S(1)} %get-tuple-element.6) | data formatting | bytes 2097152
  145.4 1.0 copy.15
  (2 shorter events, 0.0 us)
Async XLA Ops:
  7.2 51.9 %all-gather.2.cloned.1.call-start = ((), (), s32[]{:S(2)}) async-start(), calls=%async_computation.1 | async-start | bytes 2621440 | tf_op jit(solution)/shard_map/all_gather | solution.py:39
  10.3 131.6 %reduce-scatter.2.cloned.1.call-start = ((), (), s32[]{:S(2)}) async-start(), calls=%async_computation.2 | async-start | bytes 5242880 | tf_op jit(solution)/shard_map/reduce_scatter | solution.py:58
  79.3 9.0 %copy-start.1 = (s32[1,256]{1,0:T(1,128)S(1)}, s32[1,256]{1,0:T(1,128)}, u32[]{:S(2)}) copy-start(s32[1,256]{1,0:T(1,128)} %param.11) | copy-start | bytes 3076
  88.3 53.6 %copy-start = (f32[32,64,128]{2,1,0:T(8,128)S(1)}, f32[32,64,128]{2,1,0:T(8,128)}, u32[]{:S(2)}) copy-start(f32[32,64,128]{2,1,0:T(8,128)} %param.8) | copy-start | bytes 3145732
Sparse Core Ops, SparseCore 0:
  10.4 48.6 all-gather.1
  98.6 43.2 reduce-scatter.1
where the time goes:
time: 154 us; the launch traced here: 153 us
  waiting for transfers between devices  91.5 us (59%)
  local copies, waits for them, and re-layouts  23.7 us (15%)
  matrix products  18.3 us (12%)
  between operations  14.7 us (10%)
  other arithmetic  4.88 us (3%)
    all_gather x1, waiting for transfers between devices, shards(): gathered = lax.all_gather(scaled, 'col', axis=0, tiled=True)  48.1 us
    reduce_scatter x1, waiting for transfers between devices, shards(): lax.psum_scatter(partial_value, 'row', scatter_dimension=0, tiled=True)  43.4 us
    unnamed x8, local copies, waits for them, and re-layouts  14.7 us
    dot_general x1, matrix products, shards(): jnp.dot(dst_table, flat_products, precision=lax.Precision.HIGHEST, prefer...  10.2 us
    dot_general x1, local copies, waits for them, and re-layouts, shards(): jnp.dot(dst_table, flat_products, precision=lax.Precision.HIGHEST, prefer...  9.03 us
    dot_general x1, matrix products, slot_terms(): jnp.einsum('kwr,krc->kwc', picked, own_tiles, preferred_element_type=jnp....  4.72 us
    dot_general x1, matrix products, slot_terms(): jnp.dot(pick_table, sources.reshape(source_rows, width * lane_count), pre...  3.41 us
  transfers between devices with their start and end apart: 2, of which 2 were waited for; matrix products, arithmetic and copies ran while one was open for 0% of the time, Pallas kernels for 0%

commit v1 on v0

v1 whole, which is shorter than its diff:
```python
import functools

import jax
import jax.numpy as jnp
from jax import lax
from jax.experimental import pallas as pl
from jax.experimental.pallas import tpu as pltpu
from jax.sharding import PartitionSpec as P

MESH = pl.DeviceIdType.MESH
FEATS = 16
PIECES = 4


def layer_kernel(
    n_row,
    n_col,
    emb_ref,
    scale_ref,
    blocks_ref,
    perm_ref,
    src_ref,
    keep_ref,
    alive_ref,
    last_ref,
    full_ref,
    out_ref,
    tiles,
    gath,
    part,
    recv,
    running,
    blk_sem,
    ag_send,
    ag_recv,
    fw_send,
    rs_send,
    rs_recv,
):
    own = emb_ref.shape[0]
    chunks = emb_ref.shape[1] // FEATS
    slots = blocks_ref.shape[0]
    per_share = slots // n_row
    piece = slots // PIECES
    g = lax.axis_index("groups")
    r = lax.axis_index("row")
    c = lax.axis_index("col")

    def block_copy(i):
        span = pl.ds(i * piece, piece)
        return pltpu.make_async_copy(blocks_ref.at[span], tiles.at[span], blk_sem.at[i])

    for i in range(PIECES):
        block_copy(i).start()

    def row_peer(j):
        base = lax.rem(r + (j - j % 2), n_row)
        return base if j % 2 == 0 else base + 1 - 2 * lax.rem(base, 2)

    barrier = pltpu.get_barrier_semaphore()
    for d in range(1, n_col):
        pl.semaphore_signal(
            barrier, inc=1, device_id=(g, r, lax.rem(c + d, n_col)), device_id_type=MESH
        )
    for j in range(1, n_row):
        pl.semaphore_signal(barrier, inc=1, device_id=(g, row_peer(j), c), device_id_type=MESH)

    def scale_chunk(ch):
        feats = pl.ds(ch * FEATS, FEATS)
        gath[ch][pl.ds(c * own, own)] = (
            emb_ref[:, feats, :].astype(jnp.float32) * scale_ref[...]
        ).astype(jnp.bfloat16)

    for ch in range(chunks):
        scale_chunk(ch)
    pl.semaphore_wait(barrier, n_col - 1 + n_row - 1)

    def shard_copy(ch, shard, send, target):
        span = gath[ch].at[pl.ds(shard * own, own)]
        return pltpu.make_async_remote_copy(
            src_ref=span,
            dst_ref=span,
            send_sem=send,
            recv_sem=ag_recv.at[ch, shard],
            device_id=(g, r, target),
            device_id_type=MESH,
        )

    line = n_col == 4
    if line:
        near = c + 1 - 2 * lax.rem(c, 2)
        far = lax.rem(c + 2, 4)
        across = 3 - c
        inner = jnp.logical_or(c == 1, c == 2)

    def start_own(ch):
        if line:
            shard_copy(ch, c, ag_send.at[ch, 0], far).start()
            shard_copy(ch, c, ag_send.at[ch, 1], near).start()

            @pl.when(inner)
            def _():
                shard_copy(ch, c, ag_send.at[ch, 2], across).start()
        else:
            for d in range(1, n_col):
                shard_copy(ch, c, ag_send.at[ch, d - 1], lax.rem(c + d, n_col)).start()

    def await_shards(ch):
        if line:
            shard_copy(ch, far, fw_send.at[ch], near).wait_recv()

            @pl.when(inner)
            def _():
                shard_copy(ch, far, fw_send.at[ch], near).start()

    def await_rest(ch):
        if line:
            shard_copy(ch, near, fw_send.at[ch], near).wait_recv()
            shard_copy(ch, across, fw_send.at[ch], near).wait_recv()
        else:
            for d in range(1, n_col):
                shard = lax.rem(c + d, n_col)
                shard_copy(ch, shard, ag_send.at[ch, 0], shard).wait_recv()

    def finish_sends(ch):
        if line:
            shard_copy(ch, c, ag_send.at[ch, 0], far).wait_send()
            shard_copy(ch, c, ag_send.at[ch, 1], near).wait_send()

            @pl.when(inner)
            def _():
                shard_copy(ch, c, ag_send.at[ch, 2], across).wait_send()
                shard_copy(ch, far, fw_send.at[ch], near).wait_send()
        else:
            for d in range(1, n_col):
                shard_copy(ch, c, ag_send.at[ch, d - 1], lax.rem(c + d, n_col)).wait_send()

    def sum_copy(ch, j):
        return pltpu.make_async_remote_copy(
            src_ref=part.at[ch, j],
            dst_ref=recv.at[ch, j],
            send_sem=rs_send.at[ch, j],
            recv_sem=rs_recv.at[ch, j],
            device_id=(g, row_peer(j), c),
            device_id_type=MESH,
        )

    def share_sums(ch, share):
        base = share * per_share

        def slot(k, total):
            i = base + k
            x = gath[ch][src_ref[i]]
            product = jnp.dot(x, tiles[perm_ref[i]], preferred_element_type=jnp.float32)
            total = total * keep_ref[i] + product * alive_ref[i]
            running[k] = total
            return total

        lax.fori_loop(
            0, per_share, slot, jnp.zeros((FEATS, running.shape[2]), jnp.float32), unroll=16
        )

    def compute(ch):
        for j in list(range(2, n_row)) + [1, 0]:
            share = row_peer(j)
            share_sums(ch, share)

            def place(d, carry):
                i = share * own + d
                value = running[last_ref[i]] * full_ref[i]
                if j == 0:
                    out_ref[d, pl.ds(ch * FEATS, FEATS), :] = value
                else:
                    part[ch, j, d] = value.astype(jnp.bfloat16)
                return carry

            lax.fori_loop(0, own, place, 0, unroll=8)
            if j:
                sum_copy(ch, j).start()

    def reduce(ch):
        feats = pl.ds(ch * FEATS, FEATS)
        for j in range(1, n_row):
            sum_copy(ch, j).wait_recv()
        value = out_ref[:, feats, :]
        for j in range(1, n_row):
            value = value + recv[ch, j].astype(jnp.float32)
        out_ref[:, feats, :] = value

    start_own(0)
    start_own(1)
    for i in range(PIECES):
        block_copy(i).wait()
    for ch in range(chunks):
        await_shards(ch)
        if ch + 2 < chunks:
            start_own(ch + 2)
        await_rest(ch)
        compute(ch)
        if ch:
            reduce(ch - 1)
    reduce(chunks - 1)
    for ch in range(chunks):
        finish_sends(ch)
        for j in range(1, n_row):
            sum_copy(ch, j).wait_send()


def propagate(n_row, n_col, emb, scale, tiles, perm, src, keep, alive, last, full):
    own, width, lanes = emb.shape
    slots = tiles.shape[0]
    chunks = width // FEATS
    vmem = pl.BlockSpec(memory_space=pltpu.VMEM)
    smem = pl.BlockSpec(memory_space=pltpu.SMEM)
    return pl.pallas_call(
        functools.partial(layer_kernel, n_row, n_col),
        out_shape=jax.ShapeDtypeStruct((own, width, lanes), jnp.float32),
        in_specs=[vmem, vmem, pl.BlockSpec(memory_space=pl.ANY)] + [smem] * 6,
        out_specs=vmem,
        scratch_shapes=[
            pltpu.VMEM((slots, lanes, lanes), jnp.bfloat16),
            [pltpu.VMEM((n_col * own, FEATS, lanes), jnp.bfloat16) for _ in range(chunks)],
            pltpu.VMEM((chunks, n_row, own, FEATS, lanes), jnp.bfloat16),
            pltpu.VMEM((chunks, n_row, own, FEATS, lanes), jnp.bfloat16),
            pltpu.VMEM((slots // n_row, FEATS, lanes), jnp.float32),
            pltpu.SemaphoreType.DMA((PIECES,)),
            pltpu.SemaphoreType.DMA((chunks, n_col)),
            pltpu.SemaphoreType.DMA((chunks, n_col)),
            pltpu.SemaphoreType.DMA((chunks,)),
            pltpu.SemaphoreType.DMA((chunks, n_row)),
            pltpu.SemaphoreType.DMA((chunks, n_row)),
        ],
        compiler_params=pltpu.CompilerParams(
            collective_id=0, has_side_effects=True, vmem_limit_bytes=48 * 1024 * 1024
        ),
    )(emb, scale, tiles, perm, src, keep, alive, last, full)


def slot_order(rows, cols, count, n_row, own):
    slots = rows.shape[0]
    ids = jnp.arange(slots, dtype=jnp.int32)
    key = cols * slots + ids
    rank = jnp.sum((key[None, :] < key[:, None]).astype(jnp.int32), axis=1)
    hit = rank[None, :] == ids[:, None]

    def ordered(values):
        return jnp.sum(jnp.where(hit, values[None, :], 0), axis=1)

    perm = ordered(ids)
    src = ordered(rows)
    col = ordered(cols)
    alive = (perm < count).astype(jnp.float32)
    before = jnp.concatenate([jnp.full((1,), -1, jnp.int32), col[:-1]])
    keep = (before == col).astype(jnp.float32)
    dest = jnp.arange(n_row * own, dtype=jnp.int32)
    upto = jnp.sum((cols[None, :] <= dest[:, None]).astype(jnp.int32), axis=1)
    full = jnp.any(cols[None, :] == dest[:, None], axis=1).astype(jnp.float32)
    last = jnp.clip(upto - 1 - (dest // own) * (slots // n_row), 0, slots // n_row - 1)
    return perm, src, keep, alive, last, full


def shards(embedding, combined, blocks, block_rows, block_cols, block_counts, degrees):
    n_row = lax.axis_size("row")
    n_col = lax.axis_size("col")
    r = lax.axis_index("row")
    c = lax.axis_index("col")
    own, _, lanes = embedding.shape

    def root(first):
        part = lax.dynamic_slice_in_dim(degrees, first * own * lanes, own * lanes, 0)
        return (1.0 / jnp.sqrt(part.astype(jnp.float32))).reshape(own, 1, lanes)

    order = slot_order(block_rows[0], block_cols[0], block_counts[0], n_row, own)
    total = propagate(n_row, n_col, embedding, root(r * n_col + c), blocks[0], *order)
    update = total * root(c * n_row + r)
    return update.astype(jnp.bfloat16), combined + update


def solution(mesh):
    return jax.shard_map(
        shards,
        mesh=mesh,
        in_specs=(
            P(("groups", "row", "col"), None, None),
            P(("groups", "col", "row"), None, None),
            P(("groups", "row", "col"), None, None, None),
            P(("groups", "row", "col"), None),
            P(("groups", "row", "col"), None),
            P(("groups", "row", "col")),
            P("groups"),
        ),
        out_specs=(
            P(("groups", "col", "row"), None, None),
            P(("groups", "col", "row"), None, None),
        ),
        check_vma=False,
    )
```

time: 154 us -> 60.6 us (0.39)
  waiting for transfers between devices: 91.5 us -> 0 us
  Pallas kernels: 0 us -> 50.8 us
  local copies, waits for them, and re-layouts: 23.7 us -> 1.04 us
  matrix products: 18.3 us -> 0 us
  between operations: 14.7 us -> 1.34 us
    pallas_call x0 -> x1, Pallas kernels: none -> 50.8 us  [propagate(): pl.pallas_call(functools.partial(layer_kernel, n_row, n_col), out_shape=j...]
    all_gather x1 -> x0, waiting for transfers between devices: 48.1 us -> none  [shards(): gathered = lax.all_gather(scaled, 'col', axis=0, tiled=True)]
    reduce_scatter x1 -> x0, waiting for transfers between devices: 43.4 us -> none  [shards(): lax.psum_scatter(partial_value, 'row', scatter_dimension=0, tiled=True)]
    dot_general x3 -> x0, matrix products: 18.3 us -> none  [the longest x1 10.2 us: shards(): jnp.dot(dst_table, flat_products, precision=lax.Precision.HIGHEST, prefer...]
    unnamed x8 -> x4, local copies, waits for them, and re-layouts: 14.7 us -> 1.04 us
    dot_general x1 -> x0, local copies, waits for them, and re-layouts: 9.03 us -> none  [shards(): jnp.dot(dst_table, flat_products, precision=lax.Precision.HIGHEST, prefer...]
    convert_element_type x1 -> x2, other arithmetic: 1.99 us -> 0.08 us  [the longest x1 0.08 us: slot_order(): alive = (perm < count).astype(jnp.float32)]
    reduce_sum x0 -> x3, other arithmetic: none -> 1.87 us  [the longest x1 0.91 us: ordered(): return jnp.sum(jnp.where(hit, values[None, :], 0), axis=1)]
  transfers between devices with their start and end apart: 2 -> 0, of which waited for: 2 -> 0; matrix products, arithmetic and copies ran while one was open for 0% -> 0% of each run, Pallas kernels for 0% -> 0%
where the time goes in v1:
time: 60.6 us; the launch traced here: 59.5 us
  Pallas kernels  50.8 us (84%)
  other arithmetic  6.32 us (10%)
  between operations  1.34 us (2%)
  local copies, waits for them, and re-layouts  1.04 us (2%)
    pallas_call x1, Pallas kernels, propagate(): pl.pallas_call(functools.partial(layer_kernel, n_row, n_col), out_shape=j...  50.8 us
    add x1, other arithmetic, shards(): return (update.astype(jnp.bfloat16), combined + update)  1.4 us
    add x2, other arithmetic, slot_order(): key = cols * slots + ids  1.37 us

profile of v1, /device:TPU:0, one launch (start us, length us, event | category | flops | bytes accessed | tf_op | source)
XLA Modules:
  0.0 59.5 jit_solution(5784805076797973483)
XLA Ops:
  1.3 0.8 %fusion = pred[128]{0:T(512)(128)(4,1)S(1)} fusion(s32[256]{0:T(256)} %bitcast.12), kind=kLoop, calls=%fused_computation.10 | loop fusion | flops 65408 | bytes 1152 | tf_op jit(solution)/shard_map/reduce_or | solution.py:257
  2.1 0.8 %convert_reduce_fusion.1 = s32[128]{0:T(128)S(1)} fusion(s32[256]{0:T(256)} %bitcast.13), kind=kLoop, calls=%fused_computation.8 | loop fusion | flops 98176 | bytes 1536 | tf_op jit(solution)/shard_map/reduce_sum | solution.py:256
  2.9 0.7 %iota_add_fusion = s32[256]{0:T(256)S(1)} fusion(s32[256]{0:T(256)} %bitcast.14), kind=kLoop, calls=%fused_computation.19 | loop fusion | flops 512 | bytes 2048 | tf_op jit(solution)/shard_map/add | solution.py:242
  3.6 0.7 %iota_add_fusion.1 = s32[1,256]{1,0:T(1,128)S(1)} fusion(s32[1,256]{1,0:T(1,128)} %param.11), kind=kLoop, calls=%fused_computation.20 | loop fusion | flops 512 | bytes 2048 | tf_op jit(solution)/shard_map/add | solution.py:242
  4.3 0.2 convert_reduce_fusion
  4.4 0.9 %select_reduce_fusion = (s32[256]{0:T(256)S(1)}, s32[256]{0:T(256)S(1)}, s32[256]{0:T(256)S(1)}) fusion(s32[256]{0:T(256)} %bitcast.15, s32[256]{0:T(256)S(1)} %convert_reduce_fusion, s32[256]{0:T(256)} %bitcast.18), kind=kLoop, calls=%fused_computation.2 | loop fusion | flops 457984 | bytes 6144 | tf_op jit(solution)/shard_map/reduce_sum | solution.py:247
  5.4 0.1 compare_convert_fusion
  5.4 0.8 %rsqrt_bitcast_fusion = (f32[32,128]{1,0:T(8,128)S(1)}, f32[4096]{0:T(1024)S(1)}) fusion(s32[65536]{0:T(1024)} %param.13, s32[]{:T(128)S(6)} %select_n.26, s32[]{:T(128)S(6)} %select_n.21), kind=kLoop, calls=%fused_computation.11 | loop fusion | flops 8192 | bytes 65544 | tf_op jit(solution)/shard_map/mul | solution.py:275
  6.2 0.0 copy-start
  6.3 1.0 %copy-done = bf16[32,64,128]{2,1,0:T(8,128)(2,1)S(1)} copy-done((bf16[32,64,128]{2,1,0:T(8,128)(2,1)S(1)}, bf16[32,64,128]{2,1,0:T(8,128)(2,1)}, u32[]{:S(2)}) %copy-start) | copy-done | bytes 524312
  7.3 0.0 copy-start.1
  7.3 50.8 %shard_map.86 = f32[32,64,128]{2,1,0:T(8,128)S(1)} custom-call(bf16[32,64,128]{2,1,0:T(8,128)(2,1)S(1)} %copy-done, f32[32,1,128]{2,1,0:T(1,128)S(1)} %bitcast.10, bf16[256,128,128]{2,1,0:T(8,128)(2,1)} %bitcast.11, s32[256]{0:T(256)S(1)} %get-tuple-element.4.perm_ref, s32[256]{0:T(256)S(1)} %get-tuple-element.3.src_ref, f32[256]{0:T(256)S(1)} %get-tuple-element.10.keep_ref, ...), custom_call_target="tpu_custom_call" | custom-call | tf_op jit(solution)/shard_map/pallas_call | solution.py:215
  58.1 0.0 copy-done.1
  58.1 1.4 %multiply_add_fusion = (f32[32,64,128]{2,1,0:T(8,128)}, bf16[32,64,128]{2,1,0:T(8,128)(2,1)}) fusion(f32[32,64,128]{2,1,0:T(8,128)S(1)} %copy-done.1, f32[32,64,128]{2,1,0:T(8,128)S(1)} %shard_map.86, f32[32,128]{1,0:T(8,128)S(1)} %get-tuple-element.7), kind=kLoop, calls=%fused_computation | loop fusion | flops 786432 | bytes 3686400 | tf_op jit(solution)/shard_map/add | solution.py:276
  (2 shorter events, 0.0 us)
Async XLA Ops:
  6.2 1.0 %copy-start = (bf16[32,64,128]{2,1,0:T(8,128)(2,1)S(1)}, bf16[32,64,128]{2,1,0:T(8,128)(2,1)}, u32[]{:S(2)}) copy-start(bf16[32,64,128]{2,1,0:T(8,128)(2,1)} %emb_ref.1) | copy-start | bytes 1572868
  7.3 50.8 %copy-start.1 = (f32[32,64,128]{2,1,0:T(8,128)S(1)}, f32[32,64,128]{2,1,0:T(8,128)}, u32[]{:S(2)}) copy-start(f32[32,64,128]{2,1,0:T(8,128)} %param.8) | copy-start | bytes 3145732

commit v2 on v1

--- a/solution.py
+++ b/solution.py
@@ -12,33 +12,72 @@
 PIECES = 4
 
 
+def order_slots(n_row, own, rows_ref, cols_ref, count_ref, whole, real):
+    slots = rows_ref.shape[1]
+    dests = n_row * own
+    per_share = slots // n_row
+    shape = (slots, slots)
+    down = lax.broadcasted_iota(jnp.int32, shape, 0)
+    along = lax.broadcasted_iota(jnp.int32, shape, 1)
+    both = cols_ref[...] * slots + rows_ref[...]
+    both_down = jnp.sum(jnp.where(down == along, both, 0), axis=1, keepdims=True)
+    cols = cols_ref[...]
+    cols_down = both_down // slots
+    earlier = cols * slots + along < cols_down * slots + down
+    rank = jnp.sum(earlier.astype(jnp.int32), axis=1, keepdims=True)
+    same = jnp.logical_and(earlier, cols == cols_down)
+    repeats = (jnp.sum(same.astype(jnp.int32), axis=1, keepdims=True) > 0).astype(jnp.float32)
+    hit = rank == along
+    down_one = lax.broadcasted_iota(jnp.int32, (slots, 1), 0)
+    alive = (down_one < count_ref[0]).astype(jnp.float32)
+
+    def ordered(values):
+        return jnp.sum(jnp.where(hit, values, jnp.zeros_like(values)), axis=0, keepdims=True)
+
+    whole[0:1, 0:slots] = ordered(down_one)
+    whole[1:2, 0:slots] = ordered(both_down - cols_down * slots)
+    real[0:1, 0:slots] = ordered(repeats)
+    real[1:2, 0:slots] = ordered(alive)
+    dest = lax.broadcasted_iota(jnp.int32, (slots, dests), 1)
+    upto = jnp.sum((cols_down <= dest).astype(jnp.int32), axis=0, keepdims=True)
+    named = jnp.sum((cols_down == dest).astype(jnp.int32), axis=0, keepdims=True)
+    dest_one = lax.broadcasted_iota(jnp.int32, (1, dests), 1)
+    last = upto - 1 - dest_one // own * per_share
+    whole[2:3, 0:dests] = jnp.clip(last, 0, per_share - 1)
+    real[2:3, 0:dests] = (named > 0).astype(jnp.float32)
+
+
 def layer_kernel(
     n_row,
     n_col,
+    emb_hbm,
+    degree_hbm,
+    blocks_ref,
+    rows_ref,
+    cols_ref,
+    count_ref,
+    out_ref,
     emb_ref,
-    scale_ref,
-    blocks_ref,
-    perm_ref,
-    src_ref,
-    keep_ref,
-    alive_ref,
-    last_ref,
-    full_ref,
-    out_ref,
+    degree_ref,
+    whole_vmem,
+    real_vmem,
+    whole_smem,
+    real_smem,
     tiles,
     gath,
     part,
     recv,
     running,
     blk_sem,
+    in_sem,
     ag_send,
     ag_recv,
     fw_send,
     rs_send,
     rs_recv,
 ):
-    own = emb_ref.shape[0]
-    chunks = emb_ref.shape[1] // FEATS
+    own = emb_hbm.shape[0]
+    chunks = emb_hbm.shape[1] // FEATS
     slots = blocks_ref.shape[0]
     per_share = slots // n_row
     piece = slots // PIECES
@@ -50,6 +89,11 @@
         span = pl.ds(i * piece, piece)
         return pltpu.make_async_copy(blocks_ref.at[span], tiles.at[span], blk_sem.at[i])
 
+    first = (r * n_col + c) * own
+    emb_copy = pltpu.make_async_copy(emb_hbm, emb_ref, in_sem.at[0])
+    degree_copy = pltpu.make_async_copy(degree_hbm.at[pl.ds(first, own)], degree_ref, in_sem.at[1])
+    emb_copy.start()
+    degree_copy.start()
     for i in range(PIECES):
         block_copy(i).start()
 
@@ -65,10 +109,14 @@
     for j in range(1, n_row):
         pl.semaphore_signal(barrier, inc=1, device_id=(g, row_peer(j), c), device_id_type=MESH)
 
+    degree_copy.wait()
+    emb_copy.wait()
+    scale = (1.0 / jnp.sqrt(degree_ref[...].astype(jnp.float32)))[:, None, :]
+
     def scale_chunk(ch):
         feats = pl.ds(ch * FEATS, FEATS)
         gath[ch][pl.ds(c * own, own)] = (
-            emb_ref[:, feats, :].astype(jnp.float32) * scale_ref[...]
+            emb_ref[:, feats, :].astype(jnp.float32) * scale
         ).astype(jnp.bfloat16)
 
     for ch in range(chunks):
@@ -150,9 +198,9 @@
 
         def slot(k, total):
             i = base + k
-            x = gath[ch][src_ref[i]]
-            product = jnp.dot(x, tiles[perm_ref[i]], preferred_element_type=jnp.float32)
-            total = total * keep_ref[i] + product * alive_ref[i]
+            x = gath[ch][whole_smem[1, i]]
+            product = jnp.dot(x, tiles[whole_smem[0, i]], preferred_element_type=jnp.float32)
+            total = total * real_smem[0, i] + product * real_smem[1, i]
             running[k] = total
             return total
 
@@ -167,7 +215,7 @@
 
             def place(d, carry):
                 i = share * own + d
-                value = running[last_ref[i]] * full_ref[i]
+                value = running[whole_smem[2, i]] * real_smem[2, i]
                 if j == 0:
                     out_ref[d, pl.ds(ch * FEATS, FEATS), :] = value
                 else:
@@ -189,6 +237,15 @@
 
     start_own(0)
     start_own(1)
+    order_slots(n_row, own, rows_ref, cols_ref, count_ref, whole_vmem, real_vmem)
+    to_scalar = [
+        pltpu.make_async_copy(whole_vmem, whole_smem, in_sem.at[2]),
+        pltpu.make_async_copy(real_vmem, real_smem, in_sem.at[3]),
+    ]
+    for copy in to_scalar:
+        copy.start()
+    for copy in to_scalar:
+        copy.wait()
     for i in range(PIECES):
         block_copy(i).wait()
     for ch in range(chunks):
@@ -206,24 +263,32 @@
             sum_copy(ch, j).wait_send()
 
 
-def propagate(n_row, n_col, emb, scale, tiles, perm, src, keep, alive, last, full):
+def propagate(n_row, n_col, emb, degrees, tiles, rows, cols, count):
     own, width, lanes = emb.shape
     slots = tiles.shape[0]
     chunks = width // FEATS
+    table = max(slots, n_row * own)
     vmem = pl.BlockSpec(memory_space=pltpu.VMEM)
     smem = pl.BlockSpec(memory_space=pltpu.SMEM)
     return pl.pallas_call(
         functools.partial(layer_kernel, n_row, n_col),
         out_shape=jax.ShapeDtypeStruct((own, width, lanes), jnp.float32),
-        in_specs=[vmem, vmem, pl.BlockSpec(memory_space=pl.ANY)] + [smem] * 6,
+        in_specs=[pl.BlockSpec(memory_space=pl.ANY)] * 3 + [vmem, vmem, smem],
         out_specs=vmem,
         scratch_shapes=[
+            pltpu.VMEM((own, width, lanes), jnp.bfloat16),
+            pltpu.VMEM((own, lanes), jnp.int32),
+            pltpu.VMEM((8, table), jnp.int32),
+            pltpu.VMEM((8, table), jnp.float32),
+            pltpu.SMEM((8, table), jnp.int32),
+            pltpu.SMEM((8, table), jnp.float32),
             pltpu.VMEM((slots, lanes, lanes), jnp.bfloat16),
             [pltpu.VMEM((n_col * own, FEATS, lanes), jnp.bfloat16) for _ in range(chunks)],
             pltpu.VMEM((chunks, n_row, own, FEATS, lanes), jnp.bfloat16),
             pltpu.VMEM((chunks, n_row, own, FEATS, lanes), jnp.bfloat16),
             pltpu.VMEM((slots // n_row, FEATS, lanes), jnp.float32),
             pltpu.SemaphoreType.DMA((PIECES,)),
+            pltpu.SemaphoreType.DMA((4,)),
             pltpu.SemaphoreType.DMA((chunks, n_col)),
             pltpu.SemaphoreType.DMA((chunks, n_col)),
             pltpu.SemaphoreType.DMA((chunks,)),
@@ -233,30 +298,7 @@
         compiler_params=pltpu.CompilerParams(
             collective_id=0, has_side_effects=True, vmem_limit_bytes=48 * 1024 * 1024
         ),
-    )(emb, scale, tiles, perm, src, keep, alive, last, full)
-
-
-def slot_order(rows, cols, count, n_row, own):
-    slots = rows.shape[0]
-    ids = jnp.arange(slots, dtype=jnp.int32)
-    key = cols * slots + ids
-    rank = jnp.sum((key[None, :] < key[:, None]).astype(jnp.int32), axis=1)
-    hit = rank[None, :] == ids[:, None]
-
-    def ordered(values):
-        return jnp.sum(jnp.where(hit, values[None, :], 0), axis=1)
-
-    perm = ordered(ids)
-    src = ordered(rows)
-    col = ordered(cols)
-    alive = (perm < count).astype(jnp.float32)
-    before = jnp.concatenate([jnp.full((1,), -1, jnp.int32), col[:-1]])
-    keep = (before == col).astype(jnp.float32)
-    dest = jnp.arange(n_row * own, dtype=jnp.int32)
-    upto = jnp.sum((cols[None, :] <= dest[:, None]).astype(jnp.int32), axis=1)
-    full = jnp.any(cols[None, :] == dest[:, None], axis=1).astype(jnp.float32)
-    last = jnp.clip(upto - 1 - (dest // own) * (slots // n_row), 0, slots // n_row - 1)
-    return perm, src, keep, alive, last, full
+    )(emb, degrees, tiles, rows, cols, count)
 
 
 def shards(embedding, combined, blocks, block_rows, block_cols, block_counts, degrees):
@@ -266,13 +308,19 @@
     c = lax.axis_index("col")
     own, _, lanes = embedding.shape
 
-    def root(first):
-        part = lax.dynamic_slice_in_dim(degrees, first * own * lanes, own * lanes, 0)
-        return (1.0 / jnp.sqrt(part.astype(jnp.float32))).reshape(own, 1, lanes)
-
-    order = slot_order(block_rows[0], block_cols[0], block_counts[0], n_row, own)
-    total = propagate(n_row, n_col, embedding, root(r * n_col + c), blocks[0], *order)
-    update = total * root(c * n_row + r)
+    total = propagate(
+        n_row,
+        n_col,
+        embedding,
+        degrees.reshape(-1, lanes),
+        blocks[0],
+        block_rows,
+        block_cols,
+        block_counts,
+    )
+    part = lax.dynamic_slice_in_dim(degrees, (c * n_row + r) * own * lanes, own * lanes, 0)
+    root = (1.0 / jnp.sqrt(part.astype(jnp.float32))).reshape(own, 1, lanes)
+    update = total * root
     return update.astype(jnp.bfloat16), combined + update
 
 

time: 60.6 us -> 58.2 us (0.960)
  other arithmetic: 6.32 us -> 2.1 us
  local copies, waits for them, and re-layouts: 1.04 us -> 3.35 us
    unnamed x4 -> x10, local copies, waits for them, and re-layouts: 1.04 us -> 3.35 us
    reduce_sum x3 -> x0, other arithmetic: 1.87 us -> none  [the longest x1 0.91 us: ordered(): return jnp.sum(jnp.where(hit, values[None, :], 0), axis=1)]
    add x2 -> x0, other arithmetic: 1.37 us -> none  [slot_order(): key = cols * slots + ids]
    reduce_or x1 -> x0, other arithmetic: 0.79 us -> none  [slot_order(): full = jnp.any(cols[None, :] == dest[:, None], axis=1).astype(jnp.float32)]
where the time goes in v2:
time: 58.2 us; the launch traced here: 57.2 us
  Pallas kernels  50.4 us (87%)
  local copies, waits for them, and re-layouts  3.35 us (6%)
  other arithmetic  2.1 us (4%)
  between operations  1.3 us (2%)
    pallas_call x1, Pallas kernels, propagate(): pl.pallas_call(functools.partial(layer_kernel, n_row, n_col), out_shape=j...  50.4 us
    unnamed x10, local copies, waits for them, and re-layouts  3.35 us
    add x1, other arithmetic, shards(): return (update.astype(jnp.bfloat16), combined + update)  1.37 us

profile of v2, /device:TPU:0, one launch (start us, length us, event | category | flops | bytes accessed | tf_op | source)
XLA Modules:
  0.0 57.2 jit_solution(2716866572277710239)
XLA Ops:
  1.3 0.7 %rsqrt_bitcast_fusion = f32[32,128]{1,0:T(8,128)S(1)} fusion(s32[65536]{0:T(1024)} %param.13, s32[]{:T(128)S(6)} %select_n.3), kind=kLoop, calls=%fused_computation.2 | loop fusion | flops 4096 | bytes 32772 | tf_op jit(solution)/shard_map/mul | solution.py:323
  2.0 0.0 copy-start
  2.0 1.0 %copy-done = bf16[32,64,128]{2,1,0:T(8,128)(2,1)S(1)} copy-done((bf16[32,64,128]{2,1,0:T(8,128)(2,1)S(1)}, bf16[32,64,128]{2,1,0:T(8,128)(2,1)}, u32[]{:S(2)}) %copy-start) | copy-done | bytes 524312
  3.1 0.0 copy-start.1
  3.1 0.9 %copy-done.1 = s32[65536]{0:T(1024)S(1)} copy-done((s32[65536]{0:T(1024)S(1)}, s32[65536]{0:T(1024)}, u32[]{:S(2)}) %copy-start.1) | copy-done | bytes 262168
  4.0 0.0 copy-start.2
  4.0 0.7 %copy-done.2 = s32[1,256]{1,0:T(1,128)S(1)} copy-done((s32[1,256]{1,0:T(1,128)S(1)}, s32[1,256]{1,0:T(1,128)}, u32[]{:S(2)}) %copy-start.2) | copy-done | bytes 1048
  4.7 0.0 copy-start.3
  4.7 0.7 %copy-done.3 = s32[1,256]{1,0:T(1,128)S(1)} copy-done((s32[1,256]{1,0:T(1,128)S(1)}, s32[1,256]{1,0:T(1,128)}, u32[]{:S(2)}) %copy-start.3) | copy-done | bytes 1048
  5.4 0.0 copy-start.4
  5.4 50.4 %shard_map.86 = f32[32,64,128]{2,1,0:T(8,128)S(1)} custom-call(bf16[32,64,128]{2,1,0:T(8,128)(2,1)S(1)} %copy-done, s32[512,128]{1,0:T(8,128)S(1)} %bitcast.4, bf16[256,128,128]{2,1,0:T(8,128)(2,1)} %bitcast.5, s32[1,256]{1,0:T(1,128)S(1)} %copy-done.2, s32[1,256]{1,0:T(1,128)S(1)} %copy-done.3, s32[1]{0:T(128)S(6)} %copy.9.count_ref), custom_call_target="tpu_custom_call" | custom-call | tf_op jit(solution)/shard_map/pallas_call | solution.py:273
  55.8 0.0 copy-done.4
  55.8 1.4 %multiply_add_fusion = (f32[32,64,128]{2,1,0:T(8,128)}, bf16[32,64,128]{2,1,0:T(8,128)(2,1)}) fusion(f32[32,64,128]{2,1,0:T(8,128)S(1)} %copy-done.4, f32[32,64,128]{2,1,0:T(8,128)S(1)} %shard_map.86, f32[32,128]{1,0:T(8,128)S(1)} %rsqrt_bitcast_fusion), kind=kLoop, calls=%fused_computation | loop fusion | flops 786432 | bytes 3686400 | tf_op jit(solution)/shard_map/add | solution.py:324
Async XLA Ops:
  2.0 1.0 %copy-start = (bf16[32,64,128]{2,1,0:T(8,128)(2,1)S(1)}, bf16[32,64,128]{2,1,0:T(8,128)(2,1)}, u32[]{:S(2)}) copy-start(bf16[32,64,128]{2,1,0:T(8,128)(2,1)} %emb_hbm.1) | copy-start | bytes 1572868
  3.1 0.9 %copy-start.1 = (s32[65536]{0:T(1024)S(1)}, s32[65536]{0:T(1024)}, u32[]{:S(2)}) copy-start(s32[65536]{0:T(1024)} %param.13) | copy-start | bytes 786436
  4.0 0.7 %copy-start.2 = (s32[1,256]{1,0:T(1,128)S(1)}, s32[1,256]{1,0:T(1,128)}, u32[]{:S(2)}) copy-start(s32[1,256]{1,0:T(1,128)} %rows_ref.1) | copy-start | bytes 3076
  4.7 0.7 %copy-start.3 = (s32[1,256]{1,0:T(1,128)S(1)}, s32[1,256]{1,0:T(1,128)}, u32[]{:S(2)}) copy-start(s32[1,256]{1,0:T(1,128)} %cols_ref.1) | copy-start | bytes 3076
  5.4 50.4 %copy-start.4 = (f32[32,64,128]{2,1,0:T(8,128)S(1)}, f32[32,64,128]{2,1,0:T(8,128)}, u32[]{:S(2)}) copy-start(f32[32,64,128]{2,1,0:T(8,128)} %param.8) | copy-start | bytes 3145732

commit v3 on v2

--- a/solution.py
+++ b/solution.py
@@ -94,9 +94,6 @@
     degree_copy = pltpu.make_async_copy(degree_hbm.at[pl.ds(first, own)], degree_ref, in_sem.at[1])
     emb_copy.start()
     degree_copy.start()
-    for i in range(PIECES):
-        block_copy(i).start()
-
     def row_peer(j):
         base = lax.rem(r + (j - j % 2), n_row)
         return base if j % 2 == 0 else base + 1 - 2 * lax.rem(base, 2)
@@ -119,8 +116,7 @@
             emb_ref[:, feats, :].astype(jnp.float32) * scale
         ).astype(jnp.bfloat16)
 
-    for ch in range(chunks):
-        scale_chunk(ch)
+    scale_chunk(0)
     pl.semaphore_wait(barrier, n_col - 1 + n_row - 1)
 
     def shard_copy(ch, shard, send, target):
@@ -189,7 +185,7 @@
             dst_ref=recv.at[ch, j],
             send_sem=rs_send.at[ch, j],
             recv_sem=rs_recv.at[ch, j],
-            device_id=(g, row_peer(j), c),
+            device_id=(g, row_peer(1 if j % 2 else j), c),
             device_id_type=MESH,
         )
 
@@ -209,13 +205,18 @@
         )
 
     def compute(ch):
-        for j in list(range(2, n_row)) + [1, 0]:
+        pairs = [j for even in range(2, n_row, 2) for j in (even + 1, even)]
+        for j in pairs + [1, 0]:
             share = row_peer(j)
             share_sums(ch, share)
+            if j > 1 and j % 2 == 0:
+                sum_copy(ch, j + 1).wait_recv()
 
             def place(d, carry):
                 i = share * own + d
                 value = running[whole_smem[2, i]] * real_smem[2, i]
+                if j > 1 and j % 2 == 0:
+                    value = value + recv[ch, j + 1, d].astype(jnp.float32)
                 if j == 0:
                     out_ref[d, pl.ds(ch * FEATS, FEATS), :] = value
                 else:
@@ -228,15 +229,21 @@
 
     def reduce(ch):
         feats = pl.ds(ch * FEATS, FEATS)
-        for j in range(1, n_row):
+        arrivals = [1] + list(range(2, n_row, 2))
+        for j in arrivals:
             sum_copy(ch, j).wait_recv()
         value = out_ref[:, feats, :]
-        for j in range(1, n_row):
+        for j in arrivals:
             value = value + recv[ch, j].astype(jnp.float32)
         out_ref[:, feats, :] = value
 
     start_own(0)
+    scale_chunk(1)
     start_own(1)
+    for i in range(PIECES):
+        block_copy(i).start()
+    for ch in range(2, chunks):
+        scale_chunk(ch)
     order_slots(n_row, own, rows_ref, cols_ref, count_ref, whole_vmem, real_vmem)
     to_scalar = [
         pltpu.make_async_copy(whole_vmem, whole_smem, in_sem.at[2]),

time: 58.2 us -> 59.8 us (1.027); the launches traced: 57.2 us -> 59.5 us
  Pallas kernels: 50.4 us -> 52.7 us
    pallas_call x1, Pallas kernels: 50.4 us -> 52.7 us  [propagate(): pl.pallas_call(functools.partial(layer_kernel, n_row, n_col), out_shape=j...]
where the time goes in v3:
time: 59.8 us; the launch traced here: 59.5 us
  Pallas kernels  52.7 us (88%)
  local copies, waits for them, and re-layouts  3.35 us (6%)
  other arithmetic  2.1 us (4%)
  between operations  1.3 us (2%)
    pallas_call x1, Pallas kernels, propagate(): pl.pallas_call(functools.partial(layer_kernel, n_row, n_col), out_shape=j...  52.7 us
    unnamed x10, local copies, waits for them, and re-layouts  3.35 us
    add x1, other arithmetic, shards(): return (update.astype(jnp.bfloat16), combined + update)  1.37 us

profile of v3, /device:TPU:0, one launch (start us, length us, event | category | flops | bytes accessed | tf_op | source)
XLA Modules:
  0.0 59.5 jit_solution(12539639669122727460)
XLA Ops:
  1.3 0.7 %rsqrt_bitcast_fusion = f32[32,128]{1,0:T(8,128)S(1)} fusion(s32[65536]{0:T(1024)} %param.13, s32[]{:T(128)S(6)} %select_n.3), kind=kLoop, calls=%fused_computation.2 | loop fusion | flops 4096 | bytes 32772 | tf_op jit(solution)/shard_map/mul | solution.py:330
  2.0 0.0 copy-start
  2.0 1.0 %copy-done = bf16[32,64,128]{2,1,0:T(8,128)(2,1)S(1)} copy-done((bf16[32,64,128]{2,1,0:T(8,128)(2,1)S(1)}, bf16[32,64,128]{2,1,0:T(8,128)(2,1)}, u32[]{:S(2)}) %copy-start) | copy-done | bytes 524312
  3.1 0.0 copy-start.1
  3.1 0.9 %copy-done.1 = s32[65536]{0:T(1024)S(1)} copy-done((s32[65536]{0:T(1024)S(1)}, s32[65536]{0:T(1024)}, u32[]{:S(2)}) %copy-start.1) | copy-done | bytes 262168
  4.0 0.0 copy-start.2
  4.0 0.7 %copy-done.2 = s32[1,256]{1,0:T(1,128)S(1)} copy-done((s32[1,256]{1,0:T(1,128)S(1)}, s32[1,256]{1,0:T(1,128)}, u32[]{:S(2)}) %copy-start.2) | copy-done | bytes 1048
  4.7 0.0 copy-start.3
  4.7 0.7 %copy-done.3 = s32[1,256]{1,0:T(1,128)S(1)} copy-done((s32[1,256]{1,0:T(1,128)S(1)}, s32[1,256]{1,0:T(1,128)}, u32[]{:S(2)}) %copy-start.3) | copy-done | bytes 1048
  5.4 0.0 copy-start.4
  5.4 52.7 %shard_map.86 = f32[32,64,128]{2,1,0:T(8,128)S(1)} custom-call(bf16[32,64,128]{2,1,0:T(8,128)(2,1)S(1)} %copy-done, s32[512,128]{1,0:T(8,128)S(1)} %bitcast.4, bf16[256,128,128]{2,1,0:T(8,128)(2,1)} %bitcast.5, s32[1,256]{1,0:T(1,128)S(1)} %copy-done.2, s32[1,256]{1,0:T(1,128)S(1)} %copy-done.3, s32[1]{0:T(128)S(6)} %copy.9.count_ref), custom_call_target="tpu_custom_call" | custom-call | tf_op jit(solution)/shard_map/pallas_call | solution.py:280
  58.1 0.0 copy-done.4
  58.1 1.4 %multiply_add_fusion = (f32[32,64,128]{2,1,0:T(8,128)}, bf16[32,64,128]{2,1,0:T(8,128)(2,1)}) fusion(f32[32,64,128]{2,1,0:T(8,128)S(1)} %copy-done.4, f32[32,64,128]{2,1,0:T(8,128)S(1)} %shard_map.86, f32[32,128]{1,0:T(8,128)S(1)} %rsqrt_bitcast_fusion), kind=kLoop, calls=%fused_computation | loop fusion | flops 786432 | bytes 3686400 | tf_op jit(solution)/shard_map/add | solution.py:331
Async XLA Ops:
  2.0 1.0 %copy-start = (bf16[32,64,128]{2,1,0:T(8,128)(2,1)S(1)}, bf16[32,64,128]{2,1,0:T(8,128)(2,1)}, u32[]{:S(2)}) copy-start(bf16[32,64,128]{2,1,0:T(8,128)(2,1)} %emb_hbm.1) | copy-start | bytes 1572868
  3.1 0.9 %copy-start.1 = (s32[65536]{0:T(1024)S(1)}, s32[65536]{0:T(1024)}, u32[]{:S(2)}) copy-start(s32[65536]{0:T(1024)} %param.13) | copy-start | bytes 786436
  4.0 0.7 %copy-start.2 = (s32[1,256]{1,0:T(1,128)S(1)}, s32[1,256]{1,0:T(1,128)}, u32[]{:S(2)}) copy-start(s32[1,256]{1,0:T(1,128)} %rows_ref.1) | copy-start | bytes 3076
  4.7 0.7 %copy-start.3 = (s32[1,256]{1,0:T(1,128)S(1)}, s32[1,256]{1,0:T(1,128)}, u32[]{:S(2)}) copy-start(s32[1,256]{1,0:T(1,128)} %cols_ref.1) | copy-start | bytes 3076
  5.4 52.8 %copy-start.4 = (f32[32,64,128]{2,1,0:T(8,128)S(1)}, f32[32,64,128]{2,1,0:T(8,128)}, u32[]{:S(2)}) copy-start(f32[32,64,128]{2,1,0:T(8,128)} %param.8) | copy-start | bytes 3145732

commit v4 on v2

--- a/solution.py
+++ b/solution.py
@@ -205,7 +205,7 @@
             return total
 
         lax.fori_loop(
-            0, per_share, slot, jnp.zeros((FEATS, running.shape[2]), jnp.float32), unroll=16
+            0, per_share, slot, jnp.zeros((FEATS, running.shape[2]), jnp.float32), unroll=min(64, per_share)
         )
 
     def compute(ch):
@@ -222,7 +222,7 @@
                     part[ch, j, d] = value.astype(jnp.bfloat16)
                 return carry
 
-            lax.fori_loop(0, own, place, 0, unroll=8)
+            lax.fori_loop(0, own, place, 0, unroll=32)
             if j:
                 sum_copy(ch, j).start()
 

time: 58.2 us -> 56.6 us (0.973); the launches traced: 57.2 us -> 56.3 us
  Pallas kernels: 50.4 us -> 49.6 us
    pallas_call x1, Pallas kernels: 50.4 us -> 49.6 us  [propagate(): pl.pallas_call(functools.partial(layer_kernel, n_row, n_col), out_shape=j...]
where the time goes in v4:
time: 56.6 us; the launch traced here: 56.3 us
  Pallas kernels  49.6 us (88%)
  local copies, waits for them, and re-layouts  3.35 us (6%)
  other arithmetic  2.1 us (4%)
  between operations  1.3 us (2%)
    pallas_call x1, Pallas kernels, propagate(): pl.pallas_call(functools.partial(layer_kernel, n_row, n_col), out_shape=j...  49.6 us
    unnamed x10, local copies, waits for them, and re-layouts  3.35 us
    add x1, other arithmetic, shards(): return (update.astype(jnp.bfloat16), combined + update)  1.37 us

profile of v4, /device:TPU:0, one launch (start us, length us, event | category | flops | bytes accessed | tf_op | source)
XLA Modules:
  0.0 56.3 jit_solution(5416885343397736382)
XLA Ops:
  1.3 0.7 %rsqrt_bitcast_fusion = f32[32,128]{1,0:T(8,128)S(1)} fusion(s32[65536]{0:T(1024)} %param.13, s32[]{:T(128)S(6)} %select_n.3), kind=kLoop, calls=%fused_computation.2 | loop fusion | flops 4096 | bytes 32772 | tf_op jit(solution)/shard_map/mul | solution.py:323
  2.0 0.0 copy-start
  2.0 1.0 %copy-done = bf16[32,64,128]{2,1,0:T(8,128)(2,1)S(1)} copy-done((bf16[32,64,128]{2,1,0:T(8,128)(2,1)S(1)}, bf16[32,64,128]{2,1,0:T(8,128)(2,1)}, u32[]{:S(2)}) %copy-start) | copy-done | bytes 524312
  3.1 0.0 copy-start.1
  3.1 0.9 %copy-done.1 = s32[65536]{0:T(1024)S(1)} copy-done((s32[65536]{0:T(1024)S(1)}, s32[65536]{0:T(1024)}, u32[]{:S(2)}) %copy-start.1) | copy-done | bytes 262168
  4.0 0.0 copy-start.2
  4.0 0.7 %copy-done.2 = s32[1,256]{1,0:T(1,128)S(1)} copy-done((s32[1,256]{1,0:T(1,128)S(1)}, s32[1,256]{1,0:T(1,128)}, u32[]{:S(2)}) %copy-start.2) | copy-done | bytes 1048
  4.7 0.0 copy-start.3
  4.7 0.7 %copy-done.3 = s32[1,256]{1,0:T(1,128)S(1)} copy-done((s32[1,256]{1,0:T(1,128)S(1)}, s32[1,256]{1,0:T(1,128)}, u32[]{:S(2)}) %copy-start.3) | copy-done | bytes 1048
  5.4 0.0 copy-start.4
  5.4 49.6 %shard_map.86 = f32[32,64,128]{2,1,0:T(8,128)S(1)} custom-call(bf16[32,64,128]{2,1,0:T(8,128)(2,1)S(1)} %copy-done, s32[512,128]{1,0:T(8,128)S(1)} %bitcast.4, bf16[256,128,128]{2,1,0:T(8,128)(2,1)} %bitcast.5, s32[1,256]{1,0:T(1,128)S(1)} %copy-done.2, s32[1,256]{1,0:T(1,128)S(1)} %copy-done.3, s32[1]{0:T(128)S(6)} %copy.9.count_ref), custom_call_target="tpu_custom_call" | custom-call | tf_op jit(solution)/shard_map/pallas_call | solution.py:273
  54.9 0.0 copy-done.4
  54.9 1.4 %multiply_add_fusion = (f32[32,64,128]{2,1,0:T(8,128)}, bf16[32,64,128]{2,1,0:T(8,128)(2,1)}) fusion(f32[32,64,128]{2,1,0:T(8,128)S(1)} %copy-done.4, f32[32,64,128]{2,1,0:T(8,128)S(1)} %shard_map.86, f32[32,128]{1,0:T(8,128)S(1)} %rsqrt_bitcast_fusion), kind=kLoop, calls=%fused_computation | loop fusion | flops 786432 | bytes 3686400 | tf_op jit(solution)/shard_map/add | solution.py:324
Async XLA Ops:
  2.0 1.0 %copy-start = (bf16[32,64,128]{2,1,0:T(8,128)(2,1)S(1)}, bf16[32,64,128]{2,1,0:T(8,128)(2,1)}, u32[]{:S(2)}) copy-start(bf16[32,64,128]{2,1,0:T(8,128)(2,1)} %emb_hbm.1) | copy-start | bytes 1572868
  3.1 0.9 %copy-start.1 = (s32[65536]{0:T(1024)S(1)}, s32[65536]{0:T(1024)}, u32[]{:S(2)}) copy-start(s32[65536]{0:T(1024)} %param.13) | copy-start | bytes 786436
  4.0 0.7 %copy-start.2 = (s32[1,256]{1,0:T(1,128)S(1)}, s32[1,256]{1,0:T(1,128)}, u32[]{:S(2)}) copy-start(s32[1,256]{1,0:T(1,128)} %rows_ref.1) | copy-start | bytes 3076
  4.7 0.7 %copy-start.3 = (s32[1,256]{1,0:T(1,128)S(1)}, s32[1,256]{1,0:T(1,128)}, u32[]{:S(2)}) copy-start(s32[1,256]{1,0:T(1,128)} %cols_ref.1) | copy-start | bytes 3076
  5.4 49.6 %copy-start.4 = (f32[32,64,128]{2,1,0:T(8,128)S(1)}, f32[32,64,128]{2,1,0:T(8,128)}, u32[]{:S(2)}) copy-start(f32[32,64,128]{2,1,0:T(8,128)} %param.8) | copy-start | bytes 3145732

commit v5 on v4

--- a/solution.py
+++ b/solution.py
@@ -119,8 +119,7 @@
             emb_ref[:, feats, :].astype(jnp.float32) * scale
         ).astype(jnp.bfloat16)
 
-    for ch in range(chunks):
-        scale_chunk(ch)
+    scale_chunk(0)
     pl.semaphore_wait(barrier, n_col - 1 + n_row - 1)
 
     def shard_copy(ch, shard, send, target):
@@ -153,16 +152,21 @@
             for d in range(1, n_col):
                 shard_copy(ch, c, ag_send.at[ch, d - 1], lax.rem(c + d, n_col)).start()
 
-    def await_shards(ch):
+    def forward(ch):
         if line:
-            shard_copy(ch, far, fw_send.at[ch], near).wait_recv()
 
             @pl.when(inner)
             def _():
+                shard_copy(ch, far, fw_send.at[ch], near).wait_recv()
                 shard_copy(ch, far, fw_send.at[ch], near).start()
 
     def await_rest(ch):
         if line:
+
+            @pl.when(jnp.logical_not(inner))
+            def _():
+                shard_copy(ch, far, fw_send.at[ch], near).wait_recv()
+
             shard_copy(ch, near, fw_send.at[ch], near).wait_recv()
             shard_copy(ch, across, fw_send.at[ch], near).wait_recv()
         else:
@@ -236,7 +240,10 @@
         out_ref[:, feats, :] = value
 
     start_own(0)
+    scale_chunk(1)
     start_own(1)
+    for ch in range(2, chunks):
+        scale_chunk(ch)
     order_slots(n_row, own, rows_ref, cols_ref, count_ref, whole_vmem, real_vmem)
     to_scalar = [
         pltpu.make_async_copy(whole_vmem, whole_smem, in_sem.at[2]),
@@ -248,10 +255,12 @@
         copy.wait()
     for i in range(PIECES):
         block_copy(i).wait()
+    forward(0)
     for ch in range(chunks):
-        await_shards(ch)
         if ch + 2 < chunks:
             start_own(ch + 2)
+        if ch + 1 < chunks:
+            forward(ch + 1)
         await_rest(ch)
         compute(ch)
         if ch:

time: 56.6 us -> 56.5 us (level)
  Pallas kernels: 49.6 us -> 48.9 us
    pallas_call x1, Pallas kernels: 49.6 us -> 48.9 us  [propagate(): pl.pallas_call(functools.partial(layer_kernel, n_row, n_col), out_shape=j...]
where the time goes in v5:
time: 56.5 us; the launch traced here: 55.7 us
  Pallas kernels  48.9 us (87%)
  local copies, waits for them, and re-layouts  3.35 us (6%)
  other arithmetic  2.1 us (4%)
  between operations  1.3 us (2%)
    pallas_call x1, Pallas kernels, propagate(): pl.pallas_call(functools.partial(layer_kernel, n_row, n_col), out_shape=j...  48.9 us
    unnamed x10, local copies, waits for them, and re-layouts  3.35 us
    add x1, other arithmetic, shards(): return (update.astype(jnp.bfloat16), combined + update)  1.37 us

profile of v5, /device:TPU:0, one launch (start us, length us, event | category | flops | bytes accessed | tf_op | source)
XLA Modules:
  0.0 55.7 jit_solution(9487493239875319024)
XLA Ops:
  1.3 0.7 %rsqrt_bitcast_fusion = f32[32,128]{1,0:T(8,128)S(1)} fusion(s32[65536]{0:T(1024)} %param.13, s32[]{:T(128)S(6)} %select_n.3), kind=kLoop, calls=%fused_computation.2 | loop fusion | flops 4096 | bytes 32772 | tf_op jit(solution)/shard_map/mul | solution.py:332
  2.0 0.0 copy-start
  2.0 1.0 %copy-done = bf16[32,64,128]{2,1,0:T(8,128)(2,1)S(1)} copy-done((bf16[32,64,128]{2,1,0:T(8,128)(2,1)S(1)}, bf16[32,64,128]{2,1,0:T(8,128)(2,1)}, u32[]{:S(2)}) %copy-start) | copy-done | bytes 524312
  3.1 0.0 copy-start.1
  3.1 0.9 %copy-done.1 = s32[65536]{0:T(1024)S(1)} copy-done((s32[65536]{0:T(1024)S(1)}, s32[65536]{0:T(1024)}, u32[]{:S(2)}) %copy-start.1) | copy-done | bytes 262168
  4.0 0.0 copy-start.2
  4.0 0.7 %copy-done.2 = s32[1,256]{1,0:T(1,128)S(1)} copy-done((s32[1,256]{1,0:T(1,128)S(1)}, s32[1,256]{1,0:T(1,128)}, u32[]{:S(2)}) %copy-start.2) | copy-done | bytes 1048
  4.7 0.0 copy-start.3
  4.7 0.7 %copy-done.3 = s32[1,256]{1,0:T(1,128)S(1)} copy-done((s32[1,256]{1,0:T(1,128)S(1)}, s32[1,256]{1,0:T(1,128)}, u32[]{:S(2)}) %copy-start.3) | copy-done | bytes 1048
  5.4 0.0 copy-start.4
  5.4 48.9 %shard_map.86 = f32[32,64,128]{2,1,0:T(8,128)S(1)} custom-call(bf16[32,64,128]{2,1,0:T(8,128)(2,1)S(1)} %copy-done, s32[512,128]{1,0:T(8,128)S(1)} %bitcast.4, bf16[256,128,128]{2,1,0:T(8,128)(2,1)} %bitcast.5, s32[1,256]{1,0:T(1,128)S(1)} %copy-done.2, s32[1,256]{1,0:T(1,128)S(1)} %copy-done.3, s32[1]{0:T(128)S(6)} %copy.9.count_ref), custom_call_target="tpu_custom_call" | custom-call | tf_op jit(solution)/shard_map/pallas_call | solution.py:282
  54.3 0.0 copy-done.4
  54.3 1.4 %multiply_add_fusion = (f32[32,64,128]{2,1,0:T(8,128)}, bf16[32,64,128]{2,1,0:T(8,128)(2,1)}) fusion(f32[32,64,128]{2,1,0:T(8,128)S(1)} %copy-done.4, f32[32,64,128]{2,1,0:T(8,128)S(1)} %shard_map.86, f32[32,128]{1,0:T(8,128)S(1)} %rsqrt_bitcast_fusion), kind=kLoop, calls=%fused_computation | loop fusion | flops 786432 | bytes 3686400 | tf_op jit(solution)/shard_map/add | solution.py:333
Async XLA Ops:
  2.0 1.0 %copy-start = (bf16[32,64,128]{2,1,0:T(8,128)(2,1)S(1)}, bf16[32,64,128]{2,1,0:T(8,128)(2,1)}, u32[]{:S(2)}) copy-start(bf16[32,64,128]{2,1,0:T(8,128)(2,1)} %emb_hbm.1) | copy-start | bytes 1572868
  3.1 0.9 %copy-start.1 = (s32[65536]{0:T(1024)S(1)}, s32[65536]{0:T(1024)}, u32[]{:S(2)}) copy-start(s32[65536]{0:T(1024)} %param.13) | copy-start | bytes 786436
  4.0 0.7 %copy-start.2 = (s32[1,256]{1,0:T(1,128)S(1)}, s32[1,256]{1,0:T(1,128)}, u32[]{:S(2)}) copy-start(s32[1,256]{1,0:T(1,128)} %rows_ref.1) | copy-start | bytes 3076
  4.7 0.7 %copy-start.3 = (s32[1,256]{1,0:T(1,128)S(1)}, s32[1,256]{1,0:T(1,128)}, u32[]{:S(2)}) copy-start(s32[1,256]{1,0:T(1,128)} %cols_ref.1) | copy-start | bytes 3076
  5.4 48.9 %copy-start.4 = (f32[32,64,128]{2,1,0:T(8,128)S(1)}, f32[32,64,128]{2,1,0:T(8,128)}, u32[]{:S(2)}) copy-start(f32[32,64,128]{2,1,0:T(8,128)} %param.8) | copy-start | bytes 3145732
